TPU v7x, 512 devices: a whole 4x4x16 slice. The times are simulated.
512 devices in a mesh: dp: 4 (over x), ctx: 8 (over y, core), expert: 16 (over z).
Axes of the slice: x: 4, y: 4, z: 16, core: 2. Of those that a mesh axis runs over, the one named last changes fastest.
Arguments:
- tokens: bfloat16 [65536, 2048], P(('dp', 'ctx', 'expert')), parts along dimension 0, may hold values from -6 to 6
- token_tangent: bfloat16 [65536, 2048], P(('dp', 'ctx', 'expert')), parts along dimension 0, may hold values from -6 to 6
- mod_scale: float32 [8192], P('dp'), parts along dimension 0, may hold values from -1.5 to 1.5
- mod_shift: float32 [8192], P('dp'), parts along dimension 0, may hold values from -1.5 to 1.5
- scale_tangent: float32 [8192], P('dp'), parts along dimension 0, may hold values from -3 to 3
- shift_tangent: float32 [8192], P('dp'), parts along dimension 0, may hold values from -3 to 3
- out_gate: float32 [8192], P('dp'), parts along dimension 0, may hold values from 0.5 to 2
- out_gate_tangent: float32 [8192], P('dp'), parts along dimension 0, may hold values from -3 to 3
- routes: int32 [65536, 2], P(('dp', 'ctx', 'expert')), parts along dimension 0, may hold values from 0 to 15, all different within a row; in each aligned block of 128 rows (0 to 127, 128 to 255, ...) at most 32 rows name the same one
- router_gates: float32 [65536, 2], P(('dp', 'ctx', 'expert')), parts along dimension 0, may hold values from 0.05 to 0.95
- router_tangents: float32 [65536, 2], P(('dp', 'ctx', 'expert')), parts along dimension 0, may hold values from -3 to 3
- gate_weight: bfloat16 [16, 2048, 512], P('expert', 'ctx'), may hold values from -0.125 to 0.125
- up_weight: bfloat16 [16, 2048, 512], P('expert', 'ctx'), may hold values from -0.125 to 0.125
- down_weight: bfloat16 [16, 2048, 512], P('expert', 'ctx'), may hold values from -0.25 to 0.25
Outputs:
- mixed: bfloat16 [65536, 2048], P(('dp', 'ctx', 'expert')), parts along dimension 0
- mixed_tangent: bfloat16 [65536, 2048], P(('dp', 'ctx', 'expert')), parts along dimension 0
There are 4 independent parts, one for each index of `dp`. A program takes and returns all parts, laid end to end along the dimension named above; an argument that names none is the same for every part. Nothing has to cross between parts.
Inputs may be any that keep to these rules, and one draw needn't show every extreme that they name: `routes`: among the rows of one device no expert is named by more than 32 rows, a bound that some block reaches.
All inputs are finite; a program needn't handle non-finite values.
Results may differ from a plain program's by a relative error of at most 0.0059.
Values may be sent and summed in bfloat16 or wider, within the bound.
A program may use at most 64 MiB of HBM per device.

v0:
```python
import jax
import jax.numpy as jnp
from jax import lax
from jax.sharding import PartitionSpec as P


def modulate(tokens, token_tangent, mod_scale, mod_shift, scale_tangent, shift_tangent):
    primal = tokens.astype(jnp.float32)
    moving = token_tangent.astype(jnp.float32)
    inverse = lax.rsqrt(jnp.mean(primal * primal, axis=-1, keepdims=True) + 1e-06)
    normed = primal * inverse
    normed_tangent = (moving - normed * jnp.mean(normed * moving, axis=-1, keepdims=True)) * inverse
    widened = 1.0 + mod_scale
    modded = (normed * widened + mod_shift).astype(jnp.bfloat16)
    modded_tangent = (normed_tangent * widened + normed * scale_tangent + shift_tangent).astype(
        jnp.bfloat16
    )
    return (modded, modded_tangent)


def swiglu_tangent(gate_all, up_all, count):
    gate_sum, gate_move = (gate_all[:count], gate_all[count:])
    up_sum, up_move = (up_all[:count], up_all[count:])
    sigma = jax.nn.sigmoid(gate_sum)
    active = gate_sum * sigma
    slope = sigma * (1.0 + gate_sum * (1.0 - sigma))
    hidden = (active * up_sum).astype(jnp.bfloat16)
    hidden_tangent = (slope * gate_move * up_sum + active * up_move).astype(jnp.bfloat16)
    return jnp.concatenate([hidden, hidden_tangent], axis=0)


def body(
    tokens,
    token_tangent,
    mod_scale,
    mod_shift,
    scale_tangent,
    shift_tangent,
    out_gate,
    out_gate_tangent,
    routes,
    router_gates,
    router_tangents,
    gate_weight,
    up_weight,
    down_weight,
):
    n_tokens = tokens.shape[0]
    experts_total = gate_weight.shape[0] * lax.axis_size("expert")
    capacity = 4 * n_tokens // experts_total
    modded, modded_tangent = modulate(
        tokens, token_tangent, mod_scale, mod_shift, scale_tangent, shift_tangent
    )
    flat_routes = routes.reshape(-1)
    assigned = flat_routes.shape[0]
    onehot = (flat_routes[:, None] == jnp.arange(experts_total, dtype=jnp.int32)[None, :]).astype(
        jnp.int32
    )
    position = jnp.sum((jnp.cumsum(onehot, axis=0) - onehot) * onehot, axis=1)
    slots = flat_routes * capacity + position
    source = (
        jnp.full((experts_total * capacity,), assigned, jnp.int32)
        .at[slots]
        .set(jnp.arange(assigned, dtype=jnp.int32))
    )
    filled = source < assigned
    token_index = jnp.where(filled, source // 2, 0)
    blank = jnp.zeros((), jnp.bfloat16)
    send_primal = jnp.where(filled[:, None], modded[token_index], blank)
    send_tangent = jnp.where(filled[:, None], modded_tangent[token_index], blank)
    recv_primal, recv_tangent = (
        lax.all_to_all(send_primal, "expert", split_axis=0, concat_axis=0, tiled=True),
        lax.all_to_all(send_tangent, "expert", split_axis=0, concat_axis=0, tiled=True),
    )
    received = recv_primal.shape[0]
    stacked = jnp.concatenate([recv_primal, recv_tangent], axis=0)
    gate_part = jnp.dot(
        stacked,
        lax.all_gather(gate_weight, "ctx", axis=1, tiled=True)[0],
        preferred_element_type=jnp.float32,
    )
    up_part = jnp.dot(
        stacked,
        lax.all_gather(up_weight, "ctx", axis=1, tiled=True)[0],
        preferred_element_type=jnp.float32,
    )
    hidden = swiglu_tangent(gate_part, up_part, received)
    outputs = jnp.einsum(
        "rf,df->rd",
        hidden,
        lax.all_gather(down_weight, "ctx", axis=1, tiled=True)[0],
        preferred_element_type=jnp.float32,
    )
    rounded = outputs.astype(jnp.bfloat16)
    back_primal, back_tangent = (
        lax.all_to_all(rounded[:received], "expert", split_axis=0, concat_axis=0, tiled=True),
        lax.all_to_all(rounded[received:], "expert", split_axis=0, concat_axis=0, tiled=True),
    )
    picked = back_primal[slots].astype(jnp.float32).reshape(n_tokens, 2, -1)
    picked_tangent = back_tangent[slots].astype(jnp.float32).reshape(n_tokens, 2, -1)
    combined = jnp.sum(router_gates[:, :, None] * picked, axis=1)
    combined_tangent = jnp.sum(
        router_tangents[:, :, None] * picked + router_gates[:, :, None] * picked_tangent, axis=1
    )
    primal = tokens.astype(jnp.float32)
    moving = token_tangent.astype(jnp.float32)
    mixed = (primal + out_gate * combined).astype(jnp.bfloat16)
    mixed_tangent = (moving + out_gate_tangent * combined + out_gate * combined_tangent).astype(
        jnp.bfloat16
    )
    return (mixed, mixed_tangent)


def solution(mesh):
    in_specs = (
        P(("dp", "ctx", "expert"), None),
        P(("dp", "ctx", "expert"), None),
        P("dp"),
        P("dp"),
        P("dp"),
        P("dp"),
        P("dp"),
        P("dp"),
        P(("dp", "ctx", "expert"), None),
        P(("dp", "ctx", "expert"), None),
        P(("dp", "ctx", "expert"), None),
        P("expert", "ctx", None),
        P("expert", "ctx", None),
        P("expert", "ctx", None),
    )
    out_specs = (P(("dp", "ctx", "expert"), None), P(("dp", "ctx", "expert"), None))
    return jax.shard_map(body, mesh=mesh, in_specs=in_specs, out_specs=out_specs, check_vma=False)
```

profile of v0, /device:TPU:1, one launch (start us, length us, event | category | flops | bytes accessed | tf_op | source)
XLA Modules:
  0.0 481.3 jit_solution(15229232222596816153)
XLA Ops:
  10.2 1.4 scatter_custom_fusion
  11.6 1.2 fusion.13
  12.9 1.5 fusion.15
  15.1 1.3 fusion.9
  16.4 2.5 gather_fusion.1
  18.9 3.3 gather_fusion
  22.3 4.0 broadcast_select_fusion.1
  26.3 15.7 %all-to-all-start = ((bf16[16,32,2048]{2,1,0:T(8,128)(2,1)}), bf16[16,32,2048]{2,1,0:T(8,128)(2,1)S(1)}, u32[]{:S(2)}, u32[]{:S(2)}) async-start(bf16[16,32,2048]{2,1,0:T(8,128)(2,1)} %get-tuple-element.12), calls=%async_computation | async-start | bytes 4194304 | tf_op jit(solution)/shard_map/all_to_all | solution.py:72
  42.7 91.1 %all-to-all-done = bf16[16,32,2048]{2,1,0:T(8,128)(2,1)S(1)} async-done(((bf16[16,32,2048]{2,1,0:T(8,128)(2,1)}), bf16[16,32,2048]{2,1,0:T(8,128)(2,1)S(1)}, u32[]{:S(2)}, u32[]{:S(2)}) %all-to-all-start) | async-done | bytes 2097184 | tf_op jit(solution)/shard_map/all_to_all | solution.py:72
  133.9 11.2 %all-to-all-start.1 = ((bf16[16,32,2048]{2,1,0:T(8,128)(2,1)}), bf16[16,32,2048]{2,1,0:T(8,128)(2,1)}, u32[]{:S(2)}, u32[]{:S(2)}) async-start(bf16[16,32,2048]{2,1,0:T(8,128)(2,1)} %get-tuple-element.13), calls=%async_computation.1 | async-start | bytes 4194304 | tf_op jit(solution)/shard_map/all_to_all | solution.py:73
  146.6 90.4 %all-to-all-done.1 = bf16[16,32,2048]{2,1,0:T(8,128)(2,1)} async-done(((bf16[16,32,2048]{2,1,0:T(8,128)(2,1)}), bf16[16,32,2048]{2,1,0:T(8,128)(2,1)}, u32[]{:S(2)}, u32[]{:S(2)}) %all-to-all-start.1) | async-done | bytes 2097184 | tf_op jit(solution)/shard_map/all_to_all | solution.py:73
  237.0 5.9 %fusion.1 = f32[1024,512]{1,0:T(8,128)} fusion(bf16[512,2048]{1,0:T(8,128)(2,1)} %bitcast.6, bf16[512,2048]{1,0:T(8,128)(2,1)S(1)} %bitcast.44, bf16[1,2048,512]{2,1,0:T(8,128)(2,1)} %all-gather.4.cloned.1.call-done), kind=kOutput, calls=%fused_computation.8 | convolution fusion | flops 2155872256 | bytes 8388608 | tf_op jit(solution)/shard_map/dot_general | solution.py:77
  242.9 4.7 fusion
  248.2 4.0 convolution_convert_fusion
  252.2 1.9 fusion.39
  254.1 101.3 %all_to_all.42 = bf16[16,32,2048]{2,1,0:T(8,128)(2,1)} all-to-all(bf16[16,32,2048]{2,1,0:T(8,128)(2,1)S(1)} %bitcast.43), channel_id=1, replica_groups=mesh['dp'=4,'ctx'=8,'expert'=16] {'expert'}, dimensions={0} | all-to-all | bytes 4194304 | tf_op jit(solution)/shard_map/all_to_all | solution.py:96
  355.3 12.9 %all-to-all-start.3 = ((bf16[16,32,2048]{2,1,0:T(8,128)(2,1)}), bf16[16,32,2048]{2,1,0:T(8,128)(2,1)S(1)}, u32[]{:S(2)}, u32[]{:S(2)}) async-start(bf16[16,32,2048]{2,1,0:T(8,128)(2,1)} %bitcast.42), calls=%async_computation.3 | async-start | bytes 4194304 | tf_op jit(solution)/shard_map/all_to_all | solution.py:97
  368.5 4.2 gather_fusion.2
  372.7 2.3 reshape.99
  375.0 85.1 %all-to-all-done.3 = bf16[16,32,2048]{2,1,0:T(8,128)(2,1)S(1)} async-done(((bf16[16,32,2048]{2,1,0:T(8,128)(2,1)}), bf16[16,32,2048]{2,1,0:T(8,128)(2,1)S(1)}, u32[]{:S(2)}, u32[]{:S(2)}) %all-to-all-start.3) | async-done | bytes 2097184 | tf_op jit(solution)/shard_map/all_to_all | solution.py:97
  460.1 1.4 gather_fusion.3
  461.5 2.4 reshape.100
  463.8 9.6 %add_reduce_fusion = (f32[128,2048]{1,0:T(8,128)S(1)}, f32[128,2048]{1,0:T(8,128)S(1)}) fusion(f32[128,2,2048]{2,1,0:T(2,128)} %reshape.100, f32[128,2,2048]{2,1,0:T(2,128)S(1)} %copy-done, f32[128,2]{1,0:T(8,128)S(1)} %copy.23, f32[128,2]{1,0:T(8,128)S(1)} %copy.18), kind=kLoop, calls=%fused_computation.12 | loop fusion | flops 2621440 | bytes 6293504 | tf_op jit(solution)/shard_map/reduce_sum | solution.py:102
  473.5 1.3 fusion.19
  (54 shorter events, 6.9 us)
Async XLA Ops:
  7.2 8.0 %copy-start.1 = (bf16[128,2048]{1,0:T(8,128)(2,1)S(1)}, bf16[128,2048]{1,0:T(8,128)(2,1)}, u32[]{:S(2)}) copy-start(bf16[128,2048]{1,0:T(8,128)(2,1)} %param.14) | copy-start | bytes 1572868
  7.2 8.0 %copy-start.3 = (bf16[128,2048]{1,0:T(8,128)(2,1)S(1)}, bf16[128,2048]{1,0:T(8,128)(2,1)}, u32[]{:S(2)}) copy-start(bf16[128,2048]{1,0:T(8,128)(2,1)} %param.15) | copy-start | bytes 1572868
  26.3 107.6 %all-to-all-start = ((bf16[16,32,2048]{2,1,0:T(8,128)(2,1)}), bf16[16,32,2048]{2,1,0:T(8,128)(2,1)S(1)}, u32[]{:S(2)}, u32[]{:S(2)}) async-start(bf16[16,32,2048]{2,1,0:T(8,128)(2,1)} %get-tuple-element.12), calls=%async_computation | async-start | bytes 4194304 | tf_op jit(solution)/shard_map/all_to_all | solution.py:72
  42.0 104.6 %all-gather.4.cloned.1.call-start = ((), (), s32[]{:S(2)}) async-start(), calls=%async_computation.4 | async-start | bytes 2359296 | tf_op jit(solution)/shard_map/all_gather | solution.py:79
  133.9 103.1 %all-to-all-start.1 = ((bf16[16,32,2048]{2,1,0:T(8,128)(2,1)}), bf16[16,32,2048]{2,1,0:T(8,128)(2,1)}, u32[]{:S(2)}, u32[]{:S(2)}) async-start(bf16[16,32,2048]{2,1,0:T(8,128)(2,1)} %get-tuple-element.13), calls=%async_computation.1 | async-start | bytes 4194304 | tf_op jit(solution)/shard_map/all_to_all | solution.py:73
  145.1 97.8 %all-gather.6.cloned.1.call-start = ((), (), s32[]{:S(2)}) async-start(), calls=%async_computation.5 | async-start | bytes 2359296 | tf_op jit(solution)/shard_map/all_gather | solution.py:84
  145.8 102.4 %all-gather.8.cloned.1.call-start = ((), (), s32[]{:S(2)}) async-start(), calls=%async_computation.6 | async-start | bytes 2359296 | tf_op jit(solution)/shard_map/all_gather | solution.py:91
  242.9 4.7 copy-start.5
  355.3 12.9 %copy-start.8 = (f32[128,2]{0,1:T(2,128)S(1)}, f32[128,2]{0,1:T(2,128)}, u32[]{:S(2)}) copy-start(f32[128,2]{0,1:T(2,128)} %param.23) | copy-start | bytes 3076
  355.3 13.0 %copy-start.9 = (f32[128,2]{0,1:T(2,128)S(1)}, f32[128,2]{0,1:T(2,128)}, u32[]{:S(2)}) copy-start(f32[128,2]{0,1:T(2,128)} %param.24) | copy-start | bytes 3076
  355.3 104.7 %all-to-all-start.3 = ((bf16[16,32,2048]{2,1,0:T(8,128)(2,1)}), bf16[16,32,2048]{2,1,0:T(8,128)(2,1)S(1)}, u32[]{:S(2)}, u32[]{:S(2)}) async-start(bf16[16,32,2048]{2,1,0:T(8,128)(2,1)} %bitcast.42), calls=%async_computation.3 | async-start | bytes 4194304 | tf_op jit(solution)/shard_map/all_to_all | solution.py:97
  461.4 2.4 copy-start
  463.8 9.6 %copy-start.2 = (bf16[128,2048]{1,0:T(8,128)(2,1)S(1)}, bf16[128,2048]{1,0:T(8,128)(2,1)}, u32[]{:S(2)}) copy-start(bf16[128,2048]{1,0:T(8,128)(2,1)} %param.14) | copy-start | bytes 1572868
  463.8 9.6 %copy-start.4 = (bf16[128,2048]{1,0:T(8,128)(2,1)S(1)}, bf16[128,2048]{1,0:T(8,128)(2,1)}, u32[]{:S(2)}) copy-start(bf16[128,2048]{1,0:T(8,128)(2,1)} %param.15) | copy-start | bytes 1572868
  463.8 9.6 %copy-start.6 = (f32[2048]{0:T(1024)S(1)}, f32[2048]{0:T(1024)}, u32[]{:S(2)}) copy-start(f32[2048]{0:T(1024)} %param.21) | copy-start | bytes 24580
  463.8 9.6 %copy-start.7 = (f32[2048]{0:T(1024)S(1)}, f32[2048]{0:T(1024)}, u32[]{:S(2)}) copy-start(f32[2048]{0:T(1024)} %param.20) | copy-start | bytes 24580
Sparse Core Ops, SparseCore 0:
  45.0 34.8 all-gather.3
  148.1 34.6 all-gather.5
  184.9 33.2 all-gather.7
where the time goes:
time: 485 us; the launch traced here: 481 us
  waiting for transfers between devices  269 us (55%)
  blocking collectives  101 us (21%)
  starting transfers between devices  39.9 us (8%)
  other arithmetic  21.6 us (4%)
  local copies, waits for them, and re-layouts  21.3 us (4%)
  matrix products  14.5 us (3%)
  between operations  14 us (3%)
    all_to_all x1, blocking collectives, body(): lax.all_to_all(rounded[:received], 'expert', split_axis=0, concat_axis=0,...  101 us
    all_to_all x1, waiting for transfers between devices, body(): lax.all_to_all(send_primal, 'expert', split_axis=0, concat_axis=0, tiled=...  91.1 us
    all_to_all x1, waiting for transfers between devices, body(): lax.all_to_all(send_tangent, 'expert', split_axis=0, concat_axis=0, tiled...  90.4 us
    all_to_all x1, waiting for transfers between devices, body(): lax.all_to_all(rounded[received:], 'expert', split_axis=0, concat_axis=0,...  85.1 us
    all_to_all x1, starting transfers between devices, body(): lax.all_to_all(send_primal, 'expert', split_axis=0, concat_axis=0, tiled=...  15.7 us
    all_to_all x1, starting transfers between devices, body(): lax.all_to_all(rounded[received:], 'expert', split_axis=0, concat_axis=0,...  12.9 us
    all_to_all x1, starting transfers between devices, body(): lax.all_to_all(send_tangent, 'expert', split_axis=0, concat_axis=0, tiled...  11.2 us
  transfers between devices with their start and end apart: 6, of which 3 were waited for; matrix products, arithmetic and copies ran while one was open for 4% of the time, Pallas kernels for 0%

commit v1 on v0

v1 whole, which is shorter than its diff:
```python
import jax
import jax.numpy as jnp
from jax import lax
from jax.experimental import pallas as pl
from jax.experimental.pallas import tpu as pltpu
from jax.sharding import PartitionSpec as P

MESH = pl.DeviceIdType.MESH
BF16, F32 = jnp.bfloat16, jnp.float32
NX, NY, NZ = 4, 4, 16
GROUP = 2 * NX
CAP = 32
CH = 64
HOP = 3
LEAD = 8


def mod(a, n):
    return lax.rem(a + 4 * n, n)


def moe_kernel(
    tokens, tangent, vectors, routes, gates, gate_moves, gate_w, up_w, down_w,
    mixed, mixed_tangent,
    own, weights, modded, picks, packed, rows, hidden, results, returned,
    own_sem, z_sem, y_sem, x_sem, back_sem,
    seed_core, seed_y, right_sem, left_sem, side_sem, packed_sem, results_sem,
):
    n_tokens, width = tokens.shape
    pieces = 2 * NY
    piece_rows = width // pieces
    rc = piece_rows // CH
    n_first = 8 * rc
    n_all = 12 * rc
    tile = 256
    half = width // 2
    x, k, z = lax.axis_index("dp"), lax.axis_index("ctx"), lax.axis_index("expert")
    y, c = k // 2, lax.rem(k, 2)
    me = 2 * x + c

    def place(j):
        return (j // 2, 2 * y + lax.rem(j, 2), z)

    def right_distance(j):
        return mod(z - j - 1, 8) + 1

    def expert(j, s):
        return mod(z - right_distance(j) + 8 * s, NZ)

    dr = right_distance(me)
    source = (lax.rem(z, 8) // 2) == x
    taker = lax.rem(z, 2)

    loads = [
        pltpu.make_async_copy(w, own.at[i], own_sem.at[i]) for i, w in enumerate((gate_w, up_w, down_w))
    ]
    for load in loads:
        load.start()

    barrier = pltpu.get_barrier_semaphore()
    peers = [(x, k, mod(z + 1, NZ)), (x, k, mod(z - 1, NZ))]
    for step in (1, -1):
        for core in range(2):
            peers.append((x, 2 * mod(y + step, NY) + core, z))
    for other in range(1, GROUP):
        peers.append(place(lax.rem(me + other, GROUP)))
    for peer in peers:
        pl.semaphore_signal(barrier, inc=1, device_id=peer, device_id_type=MESH)
    pl.semaphore_wait(barrier, len(peers))
    for load in loads:
        load.wait()

    def send(src, dst, send_sem, recv_sem, device):
        pltpu.make_async_remote_copy(
            src_ref=src, dst_ref=dst, send_sem=send_sem, recv_sem=recv_sem, device_id=device, device_id_type=MESH
        ).start()

    def wait(ref, sem):
        pltpu.make_async_copy(ref, ref, sem).wait()

    def decode(i):
        late = i >= n_first
        i = jnp.where(late, i - n_first, i)
        a = lax.rem(i, 2)
        n = i // 2
        r = lax.rem(n, rc)
        n = n // rc
        return jnp.where(late, 2, lax.rem(n, 2)), jnp.where(late, n, n // 2), r, a

    def seed(i):
        mat, p, r, a = decode(i)

        @pl.when(source & (i < n_all) & (p == c))
        def _():
            src = own.at[mat, r]
            dst = weights.at[1, mat, (2 * y + p) * rc + r]

            @pl.when((a == 0) & (c == taker))
            def _():
                pltpu.make_async_copy(src, dst, z_sem.at[1, i]).start()

            @pl.when((a == 0) & (c != taker))
            def _():
                send(src, dst, seed_core, z_sem.at[1, i], (x, 2 * y + taker, z))

            @pl.when(a == 1)
            def _():
                send(src, dst, seed_y, z_sem.at[1, i], (x, 2 * mod(y + 1, NY) + taker, z))

    def step(t, s):
        i = t - HOP * jnp.where(s == 0, dr, 8 - dr)

        @pl.when((i >= 0) & (i < n_all))
        def _():
            mat, p, r, a = decode(i)
            row = (2 * mod(y - a, NY) + p) * rc + r
            block = weights.at[s, mat, row]
            wait(block, z_sem.at[s, i])

            @pl.when(((s == 0) & (dr < 8)) | ((s == 1) & (dr == 8)))
            def _():
                send(block, weights.at[0, mat, row], right_sem, z_sem.at[0, i], (x, k, mod(z + 1, NZ)))

            @pl.when((s == 1) & (dr != 1))
            def _():
                send(block, weights.at[1, mat, row], left_sem, z_sem.at[1, i], (x, k, mod(z - 1, NZ)))

            side = jnp.where(a == 0, mod(y - 1, NY), mod(y + 1, NY))
            phase = jnp.where(mat < 2, 0, 1 + p)
            send(block, block, side_sem, y_sem.at[s, phase], (x, 2 * side + c, z))

    def first_products(s):
        wait(rows.at[s], x_sem.at[s])
        wait(weights.at[s, 0:2, 0 : 4 * rc], y_sem.at[s, 0])

        def column(n, _):
            cols = pl.ds(pl.multiple_of(n * tile, tile), tile)
            left = rows[s].reshape(GROUP * 2 * CAP, width)
            gate = jnp.dot(left, weights[s, 0, :, :, cols].reshape(width, tile), preferred_element_type=F32)
            up = jnp.dot(left, weights[s, 1, :, :, cols].reshape(width, tile), preferred_element_type=F32)
            gate, up = gate.reshape(GROUP, 2, CAP, tile), up.reshape(GROUP, 2, CAP, tile)
            u, du, v, dv = gate[:, 0], gate[:, 1], up[:, 0], up[:, 1]
            sigma = jax.nn.sigmoid(u)
            active = u * sigma
            slope = sigma * (1.0 + u * (1.0 - sigma))
            hidden[s, :, 0, :, cols] = (active * v).astype(BF16)
            hidden[s, :, 1, :, cols] = (slope * du * v + active * dv).astype(BF16)
            return 0

        lax.fori_loop(0, hidden.shape[-1] // tile, column, 0)

    def second_products(s, p):
        wait(weights.at[s, 2, 0 : 2 * rc], y_sem.at[s, 1 + p])

        def block(n, _):
            left = hidden[s].reshape(GROUP * 2 * CAP, hidden.shape[-1])
            right = weights[s, 2, pl.ds((2 * n + p) * rc, rc)].reshape(piece_rows, hidden.shape[-1])
            out = lax.dot_general(left, right, (((1,), (1,)), ((), ())), preferred_element_type=F32)
            cols = pl.ds(pl.multiple_of(n * piece_rows, piece_rows), piece_rows)
            results[s, p, :, :, :, cols] = out.astype(BF16).reshape(GROUP, 2, CAP, piece_rows)
            return 0

        lax.fori_loop(0, NY, block, 0)
        e = expert(me, s)
        pltpu.make_async_copy(results.at[s, p, me], returned.at[p, :, e], back_sem.at[p]).start()

        def give(other, _):
            j = lax.rem(me + other, GROUP)
            send(results.at[s, p, j], returned.at[p, :, e], results_sem, back_sem.at[p], place(j))
            return 0

        lax.fori_loop(1, GROUP, give, 0)

    def ahead(i, _):
        seed(i)
        return 0

    lax.fori_loop(0, LEAD, ahead, 0)

    lanes = lax.broadcasted_iota(jnp.int32, (n_tokens, 128), 1)
    named = [lanes == routes[:, i : i + 1] for i in range(2)]
    before = lax.broadcasted_iota(jnp.int32, (n_tokens, n_tokens), 0) > lax.broadcasted_iota(
        jnp.int32, (n_tokens, n_tokens), 1
    )
    counts = jnp.dot(
        before.astype(F32).astype(BF16),
        (named[0] | named[1]).astype(F32).astype(BF16),
        preferred_element_type=F32,
    )
    slots = lax.broadcasted_iota(jnp.int32, (n_tokens, NZ * CAP), 1)
    for i in range(2):
        position = jnp.sum(jnp.where(named[i], counts, 0.0), axis=1, keepdims=True).astype(jnp.int32)
        picks[i * n_tokens : (i + 1) * n_tokens] = (
            (slots == routes[:, i : i + 1] * CAP + position).astype(F32).astype(BF16)
        )

    def modulate(n, _):
        at = pl.ds(pl.multiple_of(n * 32, 32), 32)
        primal, moving = tokens[at].astype(F32), tangent[at].astype(F32)
        inverse = lax.rsqrt(jnp.mean(primal * primal, axis=-1, keepdims=True) + 1e-06)
        normed = primal * inverse
        normed_tangent = (moving - normed * jnp.mean(normed * moving, axis=-1, keepdims=True)) * inverse
        widened = 1.0 + vectors[0:1]
        modded[0, at] = (normed * widened + vectors[1:2]).astype(BF16)
        modded[1, at] = (normed_tangent * widened + normed * vectors[2:3] + vectors[3:4]).astype(BF16)
        return 0

    lax.fori_loop(0, n_tokens // 32, modulate, 0)

    def pack(n, _):
        cols = pl.ds(pl.multiple_of(n * tile, tile), tile)
        chosen = picks[0:n_tokens] + picks[n_tokens : 2 * n_tokens]
        for i in range(2):
            out = lax.dot_general(
                chosen, modded[i, :, cols], (((0,), (0,)), ((), ())), preferred_element_type=F32
            )
            packed[:, i, :, cols] = out.astype(BF16).reshape(NZ, CAP, tile)
        return 0

    lax.fori_loop(0, width // tile, pack, 0)

    def deal(n, _):
        other = lax.rem(n, GROUP)
        j = lax.rem(me + other, GROUP)
        near = jnp.where(right_distance(j) <= 4, 0, 1)
        s = jnp.where(n < GROUP, near, 1 - near)
        e = expert(j, s)

        @pl.when(other == 0)
        def _():
            pltpu.make_async_copy(packed.at[e], rows.at[s, me], x_sem.at[s]).start()

        @pl.when(other != 0)
        def _():
            send(packed.at[e], rows.at[s, me], packed_sem, x_sem.at[s], place(j))

        return 0

    lax.fori_loop(0, 2 * GROUP, deal, 0)

    def turn(t, _):
        seed(t + LEAD)

        def stream(s, _):
            step(t, s)
            passed = t - HOP * jnp.where(s == 0, dr, 8 - dr) - HOP

            @pl.when(passed == n_first)
            def _():
                first_products(s)

            @pl.when((passed == n_first + 2 * rc) | (passed == n_all))
            def _():
                second_products(s, jnp.where(passed == n_all, 1, 0))

            return 0

        lax.fori_loop(0, 2, stream, 0)
        return 0

    lax.fori_loop(0, n_all + 9 * HOP + 1, turn, 0)

    for p in range(2):
        wait(returned.at[p], back_sem.at[p])

        def combine(n, _, p=p):
            cols = pl.ds(pl.multiple_of(n * piece_rows, piece_rows), piece_rows)
            to = pl.ds(pl.multiple_of((2 * n + p) * piece_rows, piece_rows), piece_rows)
            out, out_tangent = [
                jnp.dot(
                    picks[...],
                    returned[p, i, :, :, cols].reshape(NZ * CAP, piece_rows),
                    preferred_element_type=F32,
                )
                for i in range(2)
            ]
            g0, g1 = gates[:, 0:1], gates[:, 1:2]
            y0, y1 = out[:n_tokens], out[n_tokens:]
            total = g0 * y0 + g1 * y1
            moved = (gate_moves[:, 0:1] * y0 + g0 * out_tangent[:n_tokens]) + (
                gate_moves[:, 1:2] * y1 + g1 * out_tangent[n_tokens:]
            )
            opened, opened_move = vectors[4:5, to], vectors[5:6, to]
            mixed[:, to] = (tokens[:, to].astype(F32) + opened * total).astype(BF16)
            mixed_tangent[:, to] = (
                tangent[:, to].astype(F32) + opened_move * total + opened * moved
            ).astype(BF16)
            return 0

        lax.fori_loop(0, half // piece_rows, combine, 0)

    wait(packed.at[0 : 2 * (GROUP - 1)], packed_sem)
    wait(results.at[:, :, 0 : GROUP - 1], results_sem)
    wait(weights.at[0, :, 0 : 4 * rc], right_sem)
    wait(weights.at[:, :, 0 : 4 * rc], side_sem)

    @pl.when(dr != 1)
    def _():
        wait(weights.at[1, :, 0 : 4 * rc], left_sem)

    @pl.when(source)
    def _():
        wait(own, seed_y)

    @pl.when(source & (c != taker))
    def _():
        wait(own, seed_core)


def body(
    tokens,
    token_tangent,
    mod_scale,
    mod_shift,
    scale_tangent,
    shift_tangent,
    out_gate,
    out_gate_tangent,
    routes,
    router_gates,
    router_tangents,
    gate_weight,
    up_weight,
    down_weight,
):
    n_tokens, width = tokens.shape
    _, piece_rows, inner = gate_weight.shape
    rc = piece_rows // CH
    vectors = jnp.stack(
        [mod_scale, mod_shift, scale_tangent, shift_tangent, out_gate, out_gate_tangent, out_gate, out_gate]
    )
    shape = (rc, CH, inner)
    vmem, anywhere = pl.BlockSpec(memory_space=pltpu.VMEM), pl.BlockSpec(memory_space=pl.ANY)
    dma = pltpu.SemaphoreType.DMA
    slab = (2, CAP, width)
    return tuple(pl.pallas_call(
        moe_kernel,
        name="moe",
        out_shape=[jax.ShapeDtypeStruct(tokens.shape, BF16)] * 2,
        in_specs=[vmem] * 6 + [anywhere] * 3,
        out_specs=[vmem] * 2,
        scratch_shapes=[
            pltpu.VMEM((3, *shape), BF16),
            pltpu.VMEM((2, 3, 2 * NY * rc, CH, inner), BF16),
            pltpu.VMEM((2, n_tokens, width), BF16),
            pltpu.VMEM((2 * n_tokens, NZ * CAP), BF16),
            pltpu.VMEM((NZ, *slab), BF16),
            pltpu.VMEM((2, GROUP, *slab), BF16),
            pltpu.VMEM((2, GROUP, 2, CAP, inner), BF16),
            pltpu.VMEM((2, 2, GROUP, 2, CAP, width // 2), BF16),
            pltpu.VMEM((2, 2, NZ, CAP, width // 2), BF16),
            dma((3,)),
            dma((2, 12 * rc)),
            dma((2, 3)),
            dma((2,)),
            dma((2,)),
        ]
        + [dma] * 7,
        compiler_params=pltpu.CompilerParams(
            collective_id=0, has_side_effects=True, vmem_limit_bytes=60 * 2**20
        ),
    )(
        tokens,
        token_tangent,
        vectors,
        routes,
        router_gates,
        router_tangents,
        gate_weight.reshape(shape),
        up_weight.reshape(shape),
        down_weight.reshape(shape),
    ))


def solution(mesh):
    rows = P(("dp", "ctx", "expert"), None)
    expert_rows = P("expert", "ctx", None)
    in_specs = (rows,) * 2 + (P("dp"),) * 6 + (rows,) * 3 + (expert_rows,) * 3
    return jax.shard_map(body, mesh=mesh, in_specs=in_specs, out_specs=(rows, rows), check_vma=False)
```

time: 485 us -> 151 us (0.31)
  waiting for transfers between devices: 269 us -> 0 us
  Pallas kernels: 0 us -> 143 us
  blocking collectives: 101 us -> 0 us
  starting transfers between devices: 39.9 us -> 0 us
  other arithmetic: 21.6 us -> 0 us
  matrix products: 14.5 us -> 0 us
  local copies, waits for them, and re-layouts: 21.3 us -> 7.14 us
  between operations: 14 us -> 0.67 us
    all_to_all x3 -> x0, waiting for transfers between devices: 267 us -> none  [the longest x1 91.1 us: body(): lax.all_to_all(send_primal, 'expert', split_axis=0, concat_axis=0, tiled=...]
    pallas_call x0 -> x1, Pallas kernels: none -> 143 us  [body(): pl.pallas_call(moe_kernel, name='moe', out_shape=[jax.ShapeDtypeStruct(to...]
    all_to_all x1 -> x0, blocking collectives: 101 us -> none  [body(): lax.all_to_all(rounded[:received], 'expert', split_axis=0, concat_axis=0,...]
    all_to_all x3 -> x0, starting transfers between devices: 39.8 us -> none  [the longest x1 15.7 us: body(): lax.all_to_all(send_primal, 'expert', split_axis=0, concat_axis=0, tiled=...]
    dot_general x3 -> x0, matrix products: 14.5 us -> none  [the longest x1 5.88 us: body(): jnp.dot(stacked, lax.all_gather(gate_weight, 'ctx', axis=1, tiled=True)[0...]
    reduce_sum x4 -> x0, other arithmetic: 12.4 us -> none  [the longest x1 9.58 us: body(): jnp.sum(router_tangents[:, :, None] * picked + router_gates[:, :, None] *...]
    gather x4 -> x0, local copies, waits for them, and re-layouts: 11.4 us -> none  [the longest x1 4.22 us: body(): picked = back_primal[slots].astype(jnp.float32).reshape(n_tokens, 2, -1)]
  transfers between devices with their start and end apart: 6 -> 0, of which waited for: 3 -> 0; matrix products, arithmetic and copies ran while one was open for 4% -> 0% of each run, Pallas kernels for 0% -> 0%
where the time goes in v1:
time: 151 us
  Pallas kernels  143 us (95%)
  local copies, waits for them, and re-layouts  7.14 us (5%)
    pallas_call x1, Pallas kernels, body(): pl.pallas_call(moe_kernel, name='moe', out_shape=[jax.ShapeDtypeStruct(to...  143 us
    unnamed x17, local copies, waits for them, and re-layouts  5.66 us

profile of v1, /device:TPU:1, one launch (start us, length us, event | category | flops | bytes accessed | tf_op | source)
XLA Modules:
  0.0 151.2 jit_solution(13666559053957123030)
XLA Ops:
  0.6 0.0 copy-start.2
  0.6 0.0 copy-start.1
  0.7 0.7 copy-done.2
  1.3 0.0 copy-done.1
  1.3 0.0 copy-start.3
  1.3 1.5 stack.29.vectors
  2.8 0.0 copy-done.3
  2.8 0.0 copy-start.4
  2.8 0.7 copy.16.routes
  3.6 0.0 copy-done.4
  3.6 0.0 copy-start.5
  3.6 0.7 copy.17.gates
  4.3 0.0 copy-done.5
  4.3 0.7 copy.18.gate_moves
  5.1 143.4 %moe.1 = (bf16[128,2048]{1,0:T(8,128)(2,1)}, bf16[128,2048]{1,0:T(8,128)(2,1)}) custom-call(bf16[128,2048]{1,0:T(8,128)(2,1)} %tokens.1, bf16[128,2048]{1,0:T(8,128)(2,1)} %tangent.1, f32[8,2048]{1,0:T(8,128)} %stack.29.vectors, s32[128,2]{1,0:T(8,128)} %copy.16.routes, f32[128,2]{1,0:T(8,128)} %copy.17.gates, f32[128,2]{1,0:T(8,128)} %copy.18.gate_moves, ...), custom_call_target="tpu_custom_call" | custom-call | tf_op jit(solution)/shard_map/moe/pallas_call | solution.py:336
  148.4 0.0 copy-start
  148.4 1.9 %copy.21 = bf16[128,2048]{1,0:T(8,128)(2,1)} copy(bf16[128,2048]{1,0:T(8,128)(2,1)} %get-tuple-element.4) | data formatting | bytes 1048576
  150.4 0.0 copy-done
  150.4 0.8 copy.22
Async XLA Ops:
  0.6 0.7 copy-start.2
  0.6 0.7 copy-start.1
  1.3 1.5 copy-start.3
  2.8 0.7 copy-start.4
  3.6 0.7 copy-start.5
  148.4 2.0 %copy-start = (bf16[128,2048]{1,0:T(8,128)(2,1)S(1)}, bf16[128,2048]{1,0:T(8,128)(2,1)}, u32[]{:S(2)}) copy-start(bf16[128,2048]{1,0:T(8,128)(2,1)} %get-tuple-element.5) | copy-start | bytes 1572868

commit v2 on v1

v2 whole, which is shorter than its diff:
```python
import jax
import jax.numpy as jnp
from jax import lax
from jax.experimental import pallas as pl
from jax.experimental.pallas import tpu as pltpu
from jax.sharding import PartitionSpec as P

MESH = pl.DeviceIdType.MESH
BF16, F32 = jnp.bfloat16, jnp.float32
NX, NY, NZ = 4, 4, 16
GROUP = 2 * NX
CAP = 32
CH = 32
JOIN = 4
HOP = 6
SIDE = 3
LEAD = 8
PARTS = 4


def mod(a, n):
    return lax.rem(a + 4 * n, n)


def moe_kernel(
    tokens, tangent, scale, shift, scale_move, shift_move, opened, opened_move,
    routes, gates, gate_moves, gate_w, up_w, down_w,
    mixed, mixed_tangent,
    own, weights, modded, slots, picks, spread, packed, rows, hidden, results, returned,
    own_sem, z_sem, y_sem, x_sem, back_sem,
    seed_core, seed_y, right_sem, left_sem, side_sem, packed_sem, results_sem,
):
    n_tokens, width = tokens.shape
    pieces = 2 * NY
    piece_rows = width // pieces
    rc = piece_rows // CH
    n_first = 4 * rc
    n_all = 6 * rc
    span = width // PARTS
    strip = span // NY
    tile = 256
    x, k, z = lax.axis_index("dp"), lax.axis_index("ctx"), lax.axis_index("expert")
    y, c = k >> 1, k & 1
    me = 2 * x + c

    def place(j):
        return (j >> 1, 2 * y + (j & 1), z)

    def right_distance(j):
        return mod(z - j - 1, 8) + 1

    def expert(j, s):
        return mod(z - right_distance(j) + 8 * s, NZ)

    dr = right_distance(me)
    source = ((z & 7) >> 1) == x
    taker = z & 1

    loads = [
        pltpu.make_async_copy(w, own.at[i], own_sem.at[i]) for i, w in enumerate((gate_w, up_w, down_w))
    ]
    for load in loads:
        load.start()

    barrier = pltpu.get_barrier_semaphore()
    peers = [(x, k, mod(z + 1, NZ)), (x, k, mod(z - 1, NZ))]
    for step in (1, -1):
        for core in range(2):
            peers.append((x, 2 * mod(y + step, NY) + core, z))
    for other in range(1, GROUP):
        peers.append(place(lax.rem(me + other, GROUP)))
    for peer in peers:
        pl.semaphore_signal(barrier, inc=1, device_id=peer, device_id_type=MESH)

    pl.semaphore_wait(barrier, len(peers))
    for load in loads:
        load.wait()

    def send(src, dst, send_sem, recv_sem, device):
        pltpu.make_async_remote_copy(
            src_ref=src, dst_ref=dst, send_sem=send_sem, recv_sem=recv_sem, device_id=device, device_id_type=MESH
        ).start()

    def wait(ref, sem):
        pltpu.make_async_copy(ref, ref, sem).wait()

    ahead, behind = mod(y + 1, NY), mod(y - 1, NY)
    lag = ((HOP * dr) >> 1, (HOP * (8 - dr)) >> 1)

    def decode(j):
        n, r = lax.div(j, rc), lax.rem(j, rc)
        return n >> 1, n & 1, r, (lax.div(r, JOIN) & 1) == 1

    def seed(j):
        mat, p, r, turned = decode(j)

        @pl.when(source & (j < n_all) & (p == c))
        def _():
            src = own.at[mat, r]
            dst = weights.at[1, (8 * mat + 2 * y + p) * rc + r]

            @pl.when(c == taker)
            def _():
                pltpu.make_async_copy(src, dst, z_sem.at[1, 2 * j]).start()

            @pl.when(c != taker)
            def _():
                send(src, dst, seed_core, z_sem.at[1, 2 * j], (x, 2 * y + taker, z))

            column = jnp.where(turned, behind, ahead)
            send(src, dst, seed_y, z_sem.at[1, 2 * j + 1], (x, 2 * column + taker, z))

    def step(t, s):
        j = t - lag[s]

        @pl.when((j >= 0) & (j < n_all))
        def _():
            mat, p, r, turned = decode(j)
            base = (8 * mat + p) * rc + r
            second = jnp.where(turned, ahead, behind)
            for a, column in enumerate((y, second)):
                row = base + 2 * rc * column
                block = weights.at[s, row]
                i = 2 * j + a
                wait(block, z_sem.at[s, i])

                @pl.when(dr < 8 if s == 0 else dr == 8)
                def _():
                    send(block, weights.at[0, row], right_sem, z_sem.at[0, i], (x, k, mod(z + 1, NZ)))

                if s == 1:

                    @pl.when(dr != 1)
                    def _():
                        send(block, weights.at[1, row], left_sem, z_sem.at[1, i], (x, k, mod(z - 1, NZ)))

            @pl.when(lax.rem(r, JOIN) == JOIN - 1)
            def _():
                part = jnp.where(mat < 2, 0, 1 + lax.div(j - n_first, 2 * rc // PARTS))
                for a, column in enumerate((y, second)):
                    joined = weights.at[s, pl.ds(base + 2 * rc * column - (JOIN - 1), JOIN)]
                    side = jnp.where(turned, behind, ahead) if a else second
                    send(joined, joined, side_sem, y_sem.at[s, part], (x, 2 * side + c, z))

    def first_products(s, n):
        @pl.when(n == 0)
        def _():
            wait(rows.at[s], x_sem.at[s])
            wait(weights.at[s, 0 : 8 * rc], y_sem.at[s, 0])

        few = tile // 2
        cols = pl.ds(pl.multiple_of(n * few, few), few)
        left = rows[s].reshape(GROUP * 2 * CAP, width)
        right = jnp.concatenate(
            [weights[s, i * 8 * rc : (i + 1) * 8 * rc, :, cols].reshape(width, few) for i in range(2)], axis=1
        )
        out = jnp.dot(left, right, preferred_element_type=F32).reshape(GROUP, 2, CAP, tile)
        u, du, v, dv = out[:, 0, :, :few], out[:, 1, :, :few], out[:, 0, :, few:], out[:, 1, :, few:]
        sigma = jax.nn.sigmoid(u)
        active = u * sigma
        slope = sigma * (1.0 + u * (1.0 - sigma))
        hidden[s, :, 0, :, cols] = (active * v).astype(BF16)
        hidden[s, :, 1, :, cols] = (slope * du * v + active * dv).astype(BF16)

    def second_products(s, f):
        wait(weights.at[s, 0 : 4 * rc // PARTS], y_sem.at[s, 1 + f])
        few = strip // CH
        start = (16 + lax.div(f, PARTS // 2)) * rc + lax.rem(f, PARTS // 2) * few
        left = hidden[s].reshape(GROUP * 2 * CAP, hidden.shape[-1])
        for n in range(span // tile):
            right = jnp.concatenate(
                [
                    weights[s, pl.ds(start + 2 * rc * i, few)].reshape(strip, hidden.shape[-1])
                    for i in range(n * tile // strip, (n + 1) * tile // strip)
                ],
                axis=0,
            )
            out = lax.dot_general(left, right, (((1,), (1,)), ((), ())), preferred_element_type=F32)
            results[s, f, :, :, :, n * tile : (n + 1) * tile] = out.astype(BF16).reshape(GROUP, 2, CAP, tile)

    def give(s, f, first):
        e = expert(me, s)

        @pl.when(first == 0)
        def _():
            pltpu.make_async_copy(results.at[s, f, me], returned.at[f, :, e], back_sem.at[f]).start()

        def one(other, _):
            j = (me + other) & (GROUP - 1)
            send(results.at[s, f, j], returned.at[f, :, e], results_sem, back_sem.at[f], place(j))
            return 0

        lax.fori_loop(jnp.maximum(first, 1), first + GROUP // 2, one, 0)

    def go_ahead(j, _):
        seed(j)
        return 0

    lax.fori_loop(0, LEAD, go_ahead, 0)

    def choose(i):
        sublanes = lax.broadcasted_iota(jnp.int32, (NZ, n_tokens), 0)
        named = [sublanes == routes[j : j + 1] for j in range(2)]
        before = lax.broadcasted_iota(jnp.int32, (n_tokens, n_tokens), 0) < lax.broadcasted_iota(
            jnp.int32, (n_tokens, n_tokens), 1
        )
        counts = jnp.dot(
            (named[0] | named[1]).astype(F32).astype(BF16),
            before.astype(F32).astype(BF16),
            preferred_element_type=F32,
        )
        places = lax.broadcasted_iota(jnp.int32, (NZ * CAP, n_tokens), 0)
        position = jnp.sum(jnp.where(named[i], counts, 0.0), axis=0, keepdims=True).astype(jnp.int32)
        taken = (places == routes[i : i + 1] * CAP + position).astype(F32)
        picks[i * n_tokens : (i + 1) * n_tokens] = taken.T.astype(BF16)
        slots[...] = taken.astype(BF16) if i == 0 else slots[...] + taken.astype(BF16)
        weight = (gates, gate_moves)[i]
        for j in range(2):
            spread[2 * i + j] = jnp.broadcast_to(weight[j : j + 1], (n_tokens, n_tokens)).T

    def modulate(n):
        at = pl.ds(pl.multiple_of(n * 32, 32), 32)
        primal, moving = tokens[at].astype(F32), tangent[at].astype(F32)
        inverse = lax.rsqrt(jnp.mean(primal * primal, axis=-1, keepdims=True) + 1e-06)
        normed = primal * inverse
        normed_tangent = (moving - normed * jnp.mean(normed * moving, axis=-1, keepdims=True)) * inverse
        widened = 1.0 + scale[...]
        modded[0, at] = (normed * widened + shift[...]).astype(BF16)
        modded[1, at] = (normed_tangent * widened + normed * scale_move[...] + shift_move[...]).astype(BF16)

    def pack(n):
        cols = pl.ds(pl.multiple_of(n * 2 * tile, 2 * tile), 2 * tile)
        for i in range(2):
            out = jnp.dot(slots[...], modded[i, :, cols], preferred_element_type=F32)
            packed[:, i, :, cols] = out.astype(BF16).reshape(NZ, CAP, 2 * tile)

    def deal(n, _):
        other = lax.rem(n, GROUP)
        j = lax.rem(me + other, GROUP)
        near = jnp.where(right_distance(j) <= 4, 0, 1)
        s = jnp.where(n < GROUP, near, 1 - near)
        e = expert(j, s)

        @pl.when(other == 0)
        def _():
            pltpu.make_async_copy(packed.at[e], rows.at[s, me], x_sem.at[s]).start()

        @pl.when(other != 0)
        def _():
            send(packed.at[e], rows.at[s, me], packed_sem, x_sem.at[s], place(j))

        return 0


    n_mods, n_packs = n_tokens // 32, width // (2 * tile)

    def turn(t, _):
        seed(t + LEAD)
        step(t, 0)
        step(t, 1)

        for i in range(2):

            @pl.when(t == i)
            def _(i=i):
                choose(i)

        @pl.when((t >= 2) & (t < 2 + n_mods))
        def _():
            modulate(t - 2)

        @pl.when((t >= 2 + n_mods) & (t < 2 + n_mods + n_packs))
        def _():
            pack(t - 2 - n_mods)

        dealt = t - 2 - n_mods - n_packs

        @pl.when((dealt >= 0) & (dealt < 4))
        def _():
            lax.fori_loop(dealt * GROUP // 2, (dealt + 1) * GROUP // 2, deal, 0)

        def stream(s, _):
            u = t - jnp.where(s == 0, lag[0], lag[1]) - SIDE - n_first
            n_cols = 2 * hidden.shape[-1] // tile

            @pl.when((u >= 0) & (u < n_cols))
            def _():
                first_products(s, u)

            part_steps = 2 * rc // PARTS
            f = lax.div(u, part_steps) - 1
            at = lax.rem(u, part_steps)

            @pl.when((f >= 0) & (f < PARTS))
            def _():
                @pl.when(at == 0)
                def _():
                    second_products(s, f)

                @pl.when((at == 1) | (at == 2))
                def _():
                    give(s, f, (at - 1) * (GROUP // 2))

            return 0

        lax.fori_loop(0, 2, stream, 0)
        return 0

    lax.fori_loop(0, n_all + 4 * HOP + SIDE + 3, turn, 0)

    for f in range(PARTS):
        wait(returned.at[f], back_sem.at[f])
        for n in range(span // tile):
            out, out_tangent = [
                jnp.dot(
                    picks[...],
                    returned[f, i, :, :, n * tile : (n + 1) * tile].reshape(NZ * CAP, tile),
                    preferred_element_type=F32,
                )
                for i in range(2)
            ]
            for i in range(tile // strip):
                at = (2 * (n * tile // strip + i) + f // (PARTS // 2)) * piece_rows + f % (PARTS // 2) * strip
                to, of = slice(at, at + strip), slice(i * strip, (i + 1) * strip)
                g0, g1, m0, m1 = [
                    jnp.concatenate([spread[j]] * (strip // n_tokens), axis=1) if strip > n_tokens else spread[j]
                    for j in range(4)
                ]
                y0, y1 = out[:n_tokens, of], out[n_tokens:, of]
                total = g0 * y0 + g1 * y1
                moved = (m0 * y0 + g0 * out_tangent[:n_tokens, of]) + (m1 * y1 + g1 * out_tangent[n_tokens:, of])
                mixed[:, to] = (tokens[:, to].astype(F32) + opened[:, to] * total).astype(BF16)
                mixed_tangent[:, to] = (
                    tangent[:, to].astype(F32) + opened_move[:, to] * total + opened[:, to] * moved
                ).astype(BF16)

    wait(packed.at[0 : 2 * (GROUP - 1)], packed_sem)
    wait(results.at[:, :, 0 : GROUP - 1], results_sem)
    wait(weights.at[0, 0 : 12 * rc], right_sem)
    wait(weights.at[:, 0 : 12 * rc], side_sem)

    @pl.when(dr != 1)
    def _():
        wait(weights.at[1, 0 : 12 * rc], left_sem)

    @pl.when(source)
    def _():
        wait(own, seed_y)

    @pl.when(source & (c != taker))
    def _():
        wait(own, seed_core)


def body(
    tokens,
    token_tangent,
    mod_scale,
    mod_shift,
    scale_tangent,
    shift_tangent,
    out_gate,
    out_gate_tangent,
    routes,
    router_gates,
    router_tangents,
    gate_weight,
    up_weight,
    down_weight,
):
    n_tokens, width = tokens.shape
    _, piece_rows, inner = gate_weight.shape
    rc = piece_rows // CH
    shape = (rc, CH, inner)
    vmem, anywhere = pl.BlockSpec(memory_space=pltpu.VMEM), pl.BlockSpec(memory_space=pl.ANY)
    dma = pltpu.SemaphoreType.DMA
    slab = (2, CAP, width)
    return tuple(pl.pallas_call(
        moe_kernel,
        name="moe",
        out_shape=[jax.ShapeDtypeStruct(tokens.shape, BF16)] * 2,
        in_specs=[vmem] * 11 + [anywhere] * 3,
        out_specs=[vmem] * 2,
        scratch_shapes=[
            pltpu.VMEM((3, *shape), BF16),
            pltpu.VMEM((2, 3 * 2 * NY * rc, CH, inner), BF16),
            pltpu.VMEM((2, n_tokens, width), BF16),
            pltpu.VMEM((NZ * CAP, n_tokens), BF16),
            pltpu.VMEM((2 * n_tokens, NZ * CAP), BF16),
            pltpu.VMEM((4, n_tokens, n_tokens), F32),
            pltpu.VMEM((NZ, *slab), BF16),
            pltpu.VMEM((2, GROUP, *slab), BF16),
            pltpu.VMEM((2, GROUP, 2, CAP, inner), BF16),
            pltpu.VMEM((2, PARTS, GROUP, 2, CAP, width // PARTS), BF16),
            pltpu.VMEM((PARTS, 2, NZ, CAP, width // PARTS), BF16),
            dma((3,)),
            dma((2, 12 * rc)),
            dma((2, 1 + PARTS)),
            dma((2,)),
            dma((PARTS,)),
        ]
        + [dma] * 7,
        compiler_params=pltpu.CompilerParams(
            collective_id=0, has_side_effects=True, vmem_limit_bytes=60 * 2**20
        ),
    )(
        tokens,
        token_tangent,
        *[
            v.reshape(1, width)
            for v in (mod_scale, mod_shift, scale_tangent, shift_tangent, out_gate, out_gate_tangent)
        ],
        routes.T,
        router_gates.T,
        router_tangents.T,
        gate_weight.reshape(shape),
        up_weight.reshape(shape),
        down_weight.reshape(shape),
    ))


def solution(mesh):
    rows = P(("dp", "ctx", "expert"), None)
    expert_rows = P("expert", "ctx", None)
    in_specs = (rows,) * 2 + (P("dp"),) * 6 + (rows,) * 3 + (expert_rows,) * 3
    return jax.shard_map(body, mesh=mesh, in_specs=in_specs, out_specs=(rows, rows), check_vma=False)
```

time: 151 us -> 138 us (0.914)
  Pallas kernels: 143 us -> 134 us
  local copies, waits for them, and re-layouts: 7.14 us -> 2.74 us
    pallas_call x1, Pallas kernels: 143 us -> 134 us  [body(): pl.pallas_call(moe_kernel, name='moe', out_shape=[jax.ShapeDtypeStruct(to...]
    unnamed x17 -> x4, local copies, waits for them, and re-layouts: 5.66 us -> 2.74 us
where the time goes in v2:
time: 138 us
  Pallas kernels  134 us (97%)
  local copies, waits for them, and re-layouts  2.74 us (2%)
    pallas_call x1, Pallas kernels, body(): pl.pallas_call(moe_kernel, name='moe', out_shape=[jax.ShapeDtypeStruct(to...  134 us

profile of v2, /device:TPU:1, one launch (start us, length us, event | category | flops | bytes accessed | tf_op | source)
XLA Modules:
  0.0 137.5 jit_solution(13502983386372140099)
XLA Ops:
  0.6 134.1 %moe.1 = (bf16[128,2048]{1,0:T(8,128)(2,1)}, bf16[128,2048]{1,0:T(8,128)(2,1)}) custom-call(bf16[128,2048]{1,0:T(8,128)(2,1)} %tokens.1, bf16[128,2048]{1,0:T(8,128)(2,1)} %tangent.1, f32[1,2048]{1,0:T(1,128)} %bitcast.15, f32[1,2048]{1,0:T(1,128)} %bitcast.16, f32[1,2048]{1,0:T(1,128)} %bitcast.17, f32[1,2048]{1,0:T(1,128)} %bitcast.18, ...), custom_call_target="tpu_custom_call" | custom-call | tf_op jit(solution)/shard_map/moe/pallas_call | solution.py:378
  134.8 0.0 copy-start
  134.8 1.9 %copy.18 = bf16[128,2048]{1,0:T(8,128)(2,1)} copy(bf16[128,2048]{1,0:T(8,128)(2,1)} %get-tuple-element.4) | data formatting | bytes 1048576
  136.7 0.0 copy-done
  136.7 0.8 copy.19
Async XLA Ops:
  134.8 2.0 %copy-start = (bf16[128,2048]{1,0:T(8,128)(2,1)S(1)}, bf16[128,2048]{1,0:T(8,128)(2,1)}, u32[]{:S(2)}) copy-start(bf16[128,2048]{1,0:T(8,128)(2,1)} %get-tuple-element.5) | copy-start | bytes 1572868

commit v3 on v2

--- a/solution.py
+++ b/solution.py
@@ -11,9 +11,10 @@
 GROUP = 2 * NX
 CAP = 32
 CH = 32
-JOIN = 4
+JOIN = 2
 HOP = 6
 SIDE = 3
+DEAL = 4
 LEAD = 8
 PARTS = 4
 
@@ -23,9 +24,10 @@
 
 
 def moe_kernel(
-    tokens, tangent, scale, shift, scale_move, shift_move, opened, opened_move,
+    tokens_in, tangent_in, scale, shift, scale_move, shift_move, opened, opened_move,
     routes, gates, gate_moves, gate_w, up_w, down_w,
-    mixed, mixed_tangent,
+    mixed_out, mixed_tangent_out,
+    tokens, tangent, mixed, mixed_tangent, row_sem, out_sem,
     own, weights, modded, slots, picks, spread, packed, rows, hidden, results, returned,
     own_sem, z_sem, y_sem, x_sem, back_sem,
     seed_core, seed_y, right_sem, left_sem, side_sem, packed_sem, results_sem,
@@ -59,6 +61,10 @@
     loads = [
         pltpu.make_async_copy(w, own.at[i], own_sem.at[i]) for i, w in enumerate((gate_w, up_w, down_w))
     ]
+    loads += [
+        pltpu.make_async_copy(a, b, row_sem.at[i])
+        for i, (a, b) in enumerate(((tokens_in, tokens), (tangent_in, tangent)))
+    ]
     for load in loads:
         load.start()
 
@@ -73,7 +79,7 @@
         pl.semaphore_signal(barrier, inc=1, device_id=peer, device_id_type=MESH)
 
     pl.semaphore_wait(barrier, len(peers))
-    for load in loads:
+    for load in loads[:3]:
         load.wait()
 
     def send(src, dst, send_sem, recv_sem, device):
@@ -228,31 +234,35 @@
         modded[0, at] = (normed * widened + shift[...]).astype(BF16)
         modded[1, at] = (normed_tangent * widened + normed * scale_move[...] + shift_move[...]).astype(BF16)
 
-    def pack(n):
-        cols = pl.ds(pl.multiple_of(n * 2 * tile, 2 * tile), 2 * tile)
-        for i in range(2):
-            out = jnp.dot(slots[...], modded[i, :, cols], preferred_element_type=F32)
-            packed[:, i, :, cols] = out.astype(BF16).reshape(NZ, CAP, 2 * tile)
-
-    def deal(n, _):
-        other = lax.rem(n, GROUP)
-        j = lax.rem(me + other, GROUP)
-        near = jnp.where(right_distance(j) <= 4, 0, 1)
-        s = jnp.where(n < GROUP, near, 1 - near)
-        e = expert(j, s)
-
-        @pl.when(other == 0)
-        def _():
-            pltpu.make_async_copy(packed.at[e], rows.at[s, me], x_sem.at[s]).start()
-
-        @pl.when(other != 0)
-        def _():
-            send(packed.at[e], rows.at[s, me], packed_sem, x_sem.at[s], place(j))
-
-        return 0
-
-
-    n_mods, n_packs = n_tokens // 32, width // (2 * tile)
+    def deal(g):
+        dealt = []
+        for i in range(DEAL):
+            n = DEAL * g + i
+            j = (me + n) & (GROUP - 1)
+            near = jnp.where(right_distance(j) <= 4, 0, 1)
+            s = jnp.where(n < GROUP, near, 1 - near)
+            dealt.append((n, j, s, expert(j, s)))
+        chosen = jnp.concatenate(
+            [slots[pl.ds(pl.multiple_of(e * CAP, CAP), CAP)] for _, _, _, e in dealt], axis=0
+        )
+        for at in range(0, width, 2 * tile):
+            cols = slice(at, at + 2 * tile)
+            for i in range(2):
+                out = jnp.dot(chosen, modded[i, :, cols], preferred_element_type=F32)
+                packed[pl.ds(DEAL * g, DEAL), i, :, cols] = out.astype(BF16).reshape(DEAL, CAP, 2 * tile)
+        for i, (n, j, s, _) in enumerate(dealt):
+            if i == 0:
+
+                @pl.when(j == me)
+                def _(n=n, s=s):
+                    pltpu.make_async_copy(packed.at[n], rows.at[s, me], x_sem.at[s]).start()
+
+                @pl.when(j != me)
+                def _(n=n, s=s, j=j):
+                    send(packed.at[n], rows.at[s, me], packed_sem, x_sem.at[s], place(j))
+
+            else:
+                send(packed.at[n], rows.at[s, me], packed_sem, x_sem.at[s], place(j))
 
     def turn(t, _):
         seed(t + LEAD)
@@ -264,20 +274,16 @@
             @pl.when(t == i)
             def _(i=i):
                 choose(i)
-
-        @pl.when((t >= 2) & (t < 2 + n_mods))
-        def _():
-            modulate(t - 2)
-
-        @pl.when((t >= 2 + n_mods) & (t < 2 + n_mods + n_packs))
-        def _():
-            pack(t - 2 - n_mods)
-
-        dealt = t - 2 - n_mods - n_packs
-
-        @pl.when((dealt >= 0) & (dealt < 4))
-        def _():
-            lax.fori_loop(dealt * GROUP // 2, (dealt + 1) * GROUP // 2, deal, 0)
+                loads[3 + i].wait()
+
+        @pl.when((t >= 2) & (t < 4))
+        def _():
+            modulate(2 * t - 4)
+            modulate(2 * t - 3)
+
+        @pl.when((t >= 4) & (t < 4 + 2 * GROUP // DEAL))
+        def _():
+            deal(t - 4)
 
         def stream(s, _):
             u = t - jnp.where(s == 0, lag[0], lag[1]) - SIDE - n_first
@@ -308,6 +314,7 @@
 
     lax.fori_loop(0, n_all + 4 * HOP + SIDE + 3, turn, 0)
 
+    outs = []
     for f in range(PARTS):
         wait(returned.at[f], back_sem.at[f])
         for n in range(span // tile):
@@ -333,7 +340,15 @@
                 mixed_tangent[:, to] = (
                     tangent[:, to].astype(F32) + opened_move[:, to] * total + opened[:, to] * moved
                 ).astype(BF16)
-
+                outs += [
+                    pltpu.make_async_copy(a.at[:, to], b.at[:, to], out_sem.at[len(outs) + j])
+                    for j, (a, b) in enumerate(((mixed, mixed_out), (mixed_tangent, mixed_tangent_out)))
+                ]
+                for out_copy in outs[-2:]:
+                    out_copy.start()
+
+    for out_copy in outs:
+        out_copy.wait()
     wait(packed.at[0 : 2 * (GROUP - 1)], packed_sem)
     wait(results.at[:, :, 0 : GROUP - 1], results_sem)
     wait(weights.at[0, 0 : 12 * rc], right_sem)
@@ -379,9 +394,12 @@
         moe_kernel,
         name="moe",
         out_shape=[jax.ShapeDtypeStruct(tokens.shape, BF16)] * 2,
-        in_specs=[vmem] * 11 + [anywhere] * 3,
-        out_specs=[vmem] * 2,
-        scratch_shapes=[
+        in_specs=[anywhere] * 2 + [vmem] * 9 + [anywhere] * 3,
+        out_specs=[anywhere] * 2,
+        scratch_shapes=[pltpu.VMEM(tokens.shape, BF16)] * 4
+        + [
+            dma((2,)),
+            dma((2 * 2 * NY * 2,)),
             pltpu.VMEM((3, *shape), BF16),
             pltpu.VMEM((2, 3 * 2 * NY * rc, CH, inner), BF16),
             pltpu.VMEM((2, n_tokens, width), BF16),

time: 138 us -> 137 us (level)
  Pallas kernels: 134 us -> 132 us
    pallas_call x1, Pallas kernels: 134 us -> 132 us  [body(): pl.pallas_call(moe_kernel, name='moe', out_shape=[jax.ShapeDtypeStruct(to...]
where the time goes in v3:
time: 137 us; the launch traced here: 136 us
  Pallas kernels  132 us (96%)
  local copies, waits for them, and re-layouts  2.74 us (2%)
    pallas_call x1, Pallas kernels, body(): pl.pallas_call(moe_kernel, name='moe', out_shape=[jax.ShapeDtypeStruct(to...  132 us

profile of v3, /device:TPU:1, one launch (start us, length us, event | category | flops | bytes accessed | tf_op | source)
XLA Modules:
  0.0 135.9 jit_solution(991112726877605420)
XLA Ops:
  0.6 132.5 %moe.1 = (bf16[128,2048]{1,0:T(8,128)(2,1)}, bf16[128,2048]{1,0:T(8,128)(2,1)}) custom-call(bf16[128,2048]{1,0:T(8,128)(2,1)} %tokens_in.1, bf16[128,2048]{1,0:T(8,128)(2,1)} %tangent_in.1, f32[1,2048]{1,0:T(1,128)} %bitcast.15, f32[1,2048]{1,0:T(1,128)} %bitcast.16, f32[1,2048]{1,0:T(1,128)} %bitcast.17, f32[1,2048]{1,0:T(1,128)} %bitcast.18, ...), custom_call_target="tpu_custom_call" | custom-call | tf_op jit(solution)/shard_map/moe/pallas_call | solution.py:393
  133.1 0.0 copy-start
  133.1 1.9 %copy.18 = bf16[128,2048]{1,0:T(8,128)(2,1)} copy(bf16[128,2048]{1,0:T(8,128)(2,1)} %get-tuple-element.4) | data formatting | bytes 1048576
  135.1 0.0 copy-done
  135.1 0.8 copy.19
Async XLA Ops:
  133.1 2.0 %copy-start = (bf16[128,2048]{1,0:T(8,128)(2,1)S(1)}, bf16[128,2048]{1,0:T(8,128)(2,1)}, u32[]{:S(2)}) copy-start(bf16[128,2048]{1,0:T(8,128)(2,1)} %get-tuple-element.5) | copy-start | bytes 1572868

commit v4 on v3

--- a/solution.py
+++ b/solution.py
@@ -303,16 +303,16 @@
                 def _():
                     second_products(s, f)
 
-                @pl.when((at == 1) | (at == 2))
+                @pl.when(at < 2)
                 def _():
-                    give(s, f, (at - 1) * (GROUP // 2))
+                    give(s, f, at * (GROUP // 2))
 
             return 0
 
         lax.fori_loop(0, 2, stream, 0)
         return 0
 
-    lax.fori_loop(0, n_all + 4 * HOP + SIDE + 3, turn, 0)
+    lax.fori_loop(0, n_all + 4 * HOP + SIDE + 2, turn, 0)
 
     outs = []
     for f in range(PARTS):

time: 137 us -> 136 us (level)
  no operation moved by 1% of the time
where the time goes in v4:
time: 136 us; the launch traced here: 135 us
  Pallas kernels  132 us (97%)
  local copies, waits for them, and re-layouts  2.74 us (2%)
    pallas_call x1, Pallas kernels, body(): pl.pallas_call(moe_kernel, name='moe', out_shape=[jax.ShapeDtypeStruct(to...  132 us
    unnamed x4, local copies, waits for them, and re-layouts  2.74 us

profile of v4, /device:TPU:1, one launch (start us, length us, event | category | flops | bytes accessed | tf_op | source)
XLA Modules:
  0.0 135.0 jit_solution(15762153932352909669)
XLA Ops:
  0.6 131.6 %moe.1 = (bf16[128,2048]{1,0:T(8,128)(2,1)}, bf16[128,2048]{1,0:T(8,128)(2,1)}) custom-call(bf16[128,2048]{1,0:T(8,128)(2,1)} %tokens_in.1, bf16[128,2048]{1,0:T(8,128)(2,1)} %tangent_in.1, f32[1,2048]{1,0:T(1,128)} %bitcast.15, f32[1,2048]{1,0:T(1,128)} %bitcast.16, f32[1,2048]{1,0:T(1,128)} %bitcast.17, f32[1,2048]{1,0:T(1,128)} %bitcast.18, ...), custom_call_target="tpu_custom_call" | custom-call | tf_op jit(solution)/shard_map/moe/pallas_call | solution.py:393
  132.3 0.0 copy-start
  132.3 1.9 %copy.18 = bf16[128,2048]{1,0:T(8,128)(2,1)} copy(bf16[128,2048]{1,0:T(8,128)(2,1)} %get-tuple-element.4) | data formatting | bytes 1048576
  134.2 0.0 copy-done
  134.2 0.8 copy.19
Async XLA Ops:
  132.3 2.0 %copy-start = (bf16[128,2048]{1,0:T(8,128)(2,1)S(1)}, bf16[128,2048]{1,0:T(8,128)(2,1)}, u32[]{:S(2)}) copy-start(bf16[128,2048]{1,0:T(8,128)(2,1)} %get-tuple-element.5) | copy-start | bytes 1572868
